TPU v7x, 512 devices: a whole 4x4x16 slice. The times are simulated.
512 devices in a mesh: freq: 64 (over z_lo, x, core), lat: 8 (over z_hi, y).
Axes of the slice: x: 4, y: 4, z: 16 (z_hi: 2, z_lo: 8; z = z_hi * 8 + z_lo), core: 2. Of those that a mesh axis runs over, the one named last changes fastest.
Arguments:
- frequencies: float32 [64], P('freq'), may hold values from 0.3 to 1.5
- slowness: float32 [2, 128, 1024], P(None, 'lat', 'freq'), may hold values from 0.5 to 1.5
- src_field: float32 [64, 2, 128, 1024], P('freq', None, 'lat'), may hold values from -6 to 6
- rec_field: float32 [64, 2, 128, 1024], P('freq', None, 'lat'), may hold values from -6 to 6
Outputs:
- depth_image: float32 [2, 128, 1024], P(None, 'lat', 'freq')
- src_final: float32 [64, 2, 128, 1024], P('freq', None, 'lat')
- rec_final: float32 [64, 2, 128, 1024], P('freq', None, 'lat')
All inputs are finite; a program needn't handle non-finite values.
Results may differ from a plain program's by a relative error of at most 0.0003.
Values sent between devices are 32-bit elements; how exact they have to be, the bound alone decides.
A program may use at most 64 MiB of HBM per device.

v0:
```python
import math

import jax
import jax.numpy as jnp
from jax import lax
from jax.sharding import PartitionSpec as P

NZ = 2
TERMS = 8


step_ratio = 1.0
damping = 0.1


def extended(block, sides, width):
    for axis, dim in sides:
        count = lax.axis_size(axis)
        forward = [(i, i + 1) for i in range(count - 1)]
        backward = [(target, source) for source, target in forward]
        low = lax.ppermute(
            lax.slice_in_dim(block, block.shape[dim] - width, None, axis=dim), axis, forward
        )
        high = lax.ppermute(lax.slice_in_dim(block, 0, width, axis=dim), axis, backward)
        block = jnp.concatenate([low, block, high], axis=dim)
    return block


def neighbours(values):
    zero_col = jnp.zeros_like(values[..., :1])
    from_right = jnp.concatenate([values[..., 1:], zero_col], axis=-1)
    from_left = jnp.concatenate([zero_col, values[..., :-1]], axis=-1)
    return from_right + from_left


def mcclellan(padded):
    centre = padded[..., 1:-1, :]
    vertical = padded[..., 2:, :] + padded[..., :-2, :]
    return -0.5 * centre + 0.25 * vertical + neighbours(0.25 * centre + 0.125 * vertical)


def coefficients(wavenum, term_count):
    angles = math.pi * (jnp.arange(term_count, dtype=jnp.float32) + 0.5) / term_count
    view_shape = (term_count,) + (1,) * wavenum.ndim
    node_angles = angles.reshape(view_shape)
    excess = wavenum[None] ** 2 - node_angles**2
    absorb = damping * wavenum[None] ** 2
    modulus = jnp.sqrt(excess * excess + absorb * absorb)
    larger = jnp.sqrt(0.5 * (modulus + jnp.abs(excess)))
    smaller = absorb / (2.0 * larger)
    propagating = excess >= 0
    real_part = jnp.where(propagating, larger, smaller)
    imag_part = jnp.where(propagating, smaller, larger)
    attenuation = jnp.exp(-step_ratio * imag_part)
    phase_re = attenuation * jnp.cos(step_ratio * real_part)
    phase_im = attenuation * jnp.sin(step_ratio * real_part)
    orders = jnp.arange(term_count, dtype=jnp.float32)
    weights = jnp.where(orders == 0, 1.0, 2.0) / term_count
    cosine_table = weights[:, None] * jnp.cos(orders[:, None] * angles[None, :])
    coef_re = jnp.einsum("nj,j...->n...", cosine_table, phase_re, precision=lax.Precision.HIGHEST)
    coef_im = jnp.einsum("nj,j...->n...", cosine_table, phase_im, precision=lax.Precision.HIGHEST)
    return (coef_re, coef_im)


def accumulate(summed, coef_re, coef_im, level):
    src_re = level[..., 0, :, :]
    src_im = level[..., 1, :, :]
    rec_re = level[..., 2, :, :]
    rec_im = level[..., 3, :, :]
    term = jnp.stack(
        [
            coef_re * src_re - coef_im * src_im,
            coef_re * src_im + coef_im * src_re,
            coef_re * rec_re + coef_im * rec_im,
            coef_re * rec_im - coef_im * rec_re,
        ],
        axis=-3,
    )
    return summed + term


def raise_level(values):
    padded = extended(values, (("lat", 2),), 1)
    return mcclellan(padded)


def rim_step(wavefields, coef_re, coef_im):
    term_count = coef_re.shape[0]
    previous = wavefields
    summed = accumulate(jnp.zeros_like(wavefields), coef_re[0], coef_im[0], previous)
    current = raise_level(previous)
    summed = accumulate(summed, coef_re[1], coef_im[1], current)
    for term_index in range(2, term_count):
        following = 2.0 * raise_level(current) - previous
        summed = accumulate(summed, coef_re[term_index], coef_im[term_index], following)
        previous, current = (current, following)
    return summed


def shards(frequencies, slowness, src_field, rec_field):
    wavefields = jnp.concatenate([src_field, rec_field], axis=1)
    freq_count = lax.axis_size("freq")
    norm_factor = 1.0 / math.sqrt(wavefields.shape[0] * freq_count)
    full_slow = lax.all_gather(slowness, "freq", axis=2, tiled=True)
    partials = []
    for depth_step in range(NZ):
        slow_layer = full_slow[depth_step]
        coef_re, coef_im = coefficients(frequencies[:, None, None] * slow_layer[None], TERMS)
        wavefields = rim_step(wavefields, coef_re, coef_im)
        partial_value = jnp.sum(
            wavefields[:, 0] * wavefields[:, 2] + wavefields[:, 1] * wavefields[:, 3], axis=0
        )
        partials.append(partial_value)
    depth_image = (
        lax.psum_scatter(jnp.stack(partials), "freq", scatter_dimension=2, tiled=True) * norm_factor
    )
    return (depth_image, wavefields[:, :2], wavefields[:, 2:])


def solution(mesh):
    placed = (
        P("freq"),
        P(None, "lat", "freq"),
        P("freq", None, "lat", None),
        P("freq", None, "lat", None),
    )
    return jax.shard_map(
        shards,
        mesh=mesh,
        in_specs=placed,
        out_specs=(
            P(None, "lat", "freq"),
            P("freq", None, "lat", None),
            P("freq", None, "lat", None),
        ),
        check_vma=False,
    )
```

profile of v0, /device:TPU:24, one launch (start us, length us, event | category | flops | bytes accessed | tf_op | source)
XLA Modules:
  0.0 897.6 jit_solution(5849739694801983435)
XLA Ops:
  9.5 2.7 collective-permute-start
  12.1 14.7 %collective-permute-start.1 = (f32[1,4,1,1024]{3,0,2,1:T(1,128)S(1)}, f32[1,4,1,1024]{3,0,2,1:T(1,128)S(1)}, u32[]{:S(2)}, u32[]{:S(2)}) collective-permute-start(f32[1,4,1,1024]{3,0,2,1:T(1,128)S(1)} %get-tuple-element.141), channel_id=1, source_target_pairs={{0,1},{1,2},{2,3},{3,4},{4,5},{5,6},{6,7},{8,9},{9,10},{10,11},{11... | collective-permute-start | bytes 49160 | tf_op jit(solution)/shard_map/ppermute | solution.py:21
  28.2 127.7 %all_gather.3 = f32[2,16,1024]{1,0,2:T(2,128)S(1)} all-gather(f32[2,16,16]{1,0,2:T(2,128)S(1)} %copy.34), channel_id=1, replica_groups=mesh['freq'=64,'lat'=8] {'freq'}, dimensions={2}, use_global_device_ids=true | all-gather | bytes 133120 | tf_op jit(solution)/shard_map/all_gather | solution.py:104
  157.5 2.8 fusion.27
  160.4 2.8 fusion.24
  163.2 2.8 fusion.21
  166.2 2.8 fusion.18
  171.0 1.9 collective-permute-start.2
  172.9 14.7 %collective-permute-start.3 = (f32[1,4,1,1024]{3,0,2,1:T(1,128)S(1)}, f32[1,4,1,1024]{3,0,2,1:T(1,128)S(1)}, u32[]{:S(2)}, u32[]{:S(2)}) collective-permute-start(f32[1,4,1,1024]{3,0,2,1:T(1,128)S(1)} %get-tuple-element.137), channel_id=1, source_target_pairs={{0,1},{1,2},{2,3},{3,4},{4,5},{5,6},{6,7},{8,9},{9,10},{10,11},{11... | collective-permute-start | bytes 49160 | tf_op jit(solution)/shard_map/ppermute | solution.py:21
  191.0 1.9 collective-permute-start.4
  192.9 14.9 %collective-permute-start.5 = (f32[1,4,1,1024]{3,0,2,1:T(1,128)S(1)}, f32[1,4,1,1024]{3,0,2,1:T(1,128)S(1)}, u32[]{:S(2)}, u32[]{:S(2)}) collective-permute-start(f32[1,4,1,1024]{3,0,2,1:T(1,128)S(1)} %get-tuple-element.133), channel_id=1, source_target_pairs={{0,1},{1,2},{2,3},{3,4},{4,5},{5,6},{6,7},{8,9},{9,10},{10,11},{11... | collective-permute-start | bytes 49160 | tf_op jit(solution)/shard_map/ppermute | solution.py:21
  211.2 1.9 collective-permute-start.6
  213.1 14.9 %collective-permute-start.7 = (f32[1,4,1,1024]{3,0,2,1:T(1,128)S(1)}, f32[1,4,1,1024]{3,0,2,1:T(1,128)S(1)}, u32[]{:S(2)}, u32[]{:S(2)}) collective-permute-start(f32[1,4,1,1024]{3,0,2,1:T(1,128)S(1)} %get-tuple-element.129), channel_id=1, source_target_pairs={{0,1},{1,2},{2,3},{3,4},{4,5},{5,6},{6,7},{8,9},{9,10},{10,11},{11... | collective-permute-start | bytes 49160 | tf_op jit(solution)/shard_map/ppermute | solution.py:21
  231.3 1.9 collective-permute-start.8
  233.3 14.9 %collective-permute-start.9 = (f32[1,4,1,1024]{3,0,2,1:T(1,128)S(1)}, f32[1,4,1,1024]{3,0,2,1:T(1,128)S(1)}, u32[]{:S(2)}, u32[]{:S(2)}) collective-permute-start(f32[1,4,1,1024]{3,0,2,1:T(1,128)S(1)} %get-tuple-element.125), channel_id=1, source_target_pairs={{0,1},{1,2},{2,3},{3,4},{4,5},{5,6},{6,7},{8,9},{9,10},{10,11},{11... | collective-permute-start | bytes 49160 | tf_op jit(solution)/shard_map/ppermute | solution.py:21
  251.5 1.9 collective-permute-start.10
  253.5 15.3 %collective-permute-start.11 = (f32[1,4,1,1024]{3,0,2,1:T(1,128)S(1)}, f32[1,4,1,1024]{3,0,2,1:T(1,128)S(1)}, u32[]{:S(2)}, u32[]{:S(2)}) collective-permute-start(f32[1,4,1,1024]{3,0,2,1:T(1,128)S(1)} %get-tuple-element.121), channel_id=1, source_target_pairs={{0,1},{1,2},{2,3},{3,4},{4,5},{5,6},{6,7},{8,9},{9,10},{10,11},{11... | collective-permute-start | bytes 49160 | tf_op jit(solution)/shard_map/ppermute | solution.py:21
  272.1 1.9 collective-permute-start.12
  274.0 14.7 %collective-permute-start.13 = (f32[1,4,1,1024]{3,0,2,1:T(1,128)S(1)}, f32[1,4,1,1024]{3,0,2,1:T(1,128)S(1)}, u32[]{:S(2)}, u32[]{:S(2)}) collective-permute-start(f32[1,4,1,1024]{3,0,2,1:T(1,128)S(1)} %get-tuple-element.117), channel_id=1, source_target_pairs={{0,1},{1,2},{2,3},{3,4},{4,5},{5,6},{6,7},{8,9},{9,10},{10,11},{11... | collective-permute-start | bytes 49160 | tf_op jit(solution)/shard_map/ppermute | solution.py:21
  295.0 1.9 collective-permute-start.14
  297.0 14.9 %collective-permute-start.15 = (f32[1,4,1,1024]{3,0,2,1:T(1,128)S(1)}, f32[1,4,1,1024]{3,0,2,1:T(1,128)S(1)}, u32[]{:S(2)}, u32[]{:S(2)}) collective-permute-start(f32[1,4,1,1024]{3,0,2,1:T(1,128)S(1)} %get-tuple-element.113), channel_id=1, source_target_pairs={{0,1},{1,2},{2,3},{3,4},{4,5},{5,6},{6,7},{8,9},{9,10},{10,11},{11... | collective-permute-start | bytes 49160 | tf_op jit(solution)/shard_map/ppermute | solution.py:21
  317.0 15.0 %collective-permute-start.17 = (f32[1,4,1,1024]{3,0,2,1:T(1,128)S(1)}, f32[1,4,1,1024]{3,0,2,1:T(1,128)S(1)}, u32[]{:S(2)}, u32[]{:S(2)}) collective-permute-start(f32[1,4,1,1024]{3,0,2,1:T(1,128)S(1)} %get-tuple-element.109), channel_id=1, source_target_pairs={{0,1},{1,2},{2,3},{3,4},{4,5},{5,6},{6,7},{8,9},{9,10},{10,11},{11... | collective-permute-start | bytes 49160 | tf_op jit(solution)/shard_map/ppermute | solution.py:21
  334.4 3.3 multiply_subtract_fusion.5
  339.6 15.0 %collective-permute-start.19 = (f32[1,4,1,1024]{3,0,2,1:T(1,128)S(1)}, f32[1,4,1,1024]{3,0,2,1:T(1,128)S(1)}, u32[]{:S(2)}, u32[]{:S(2)}) collective-permute-start(f32[1,4,1,1024]{3,0,2,1:T(1,128)S(1)} %get-tuple-element.105), channel_id=1, source_target_pairs={{0,1},{1,2},{2,3},{3,4},{4,5},{5,6},{6,7},{8,9},{9,10},{10,11},{11... | collective-permute-start | bytes 49160 | tf_op jit(solution)/shard_map/ppermute | solution.py:21
  357.9 1.9 collective-permute-start.20
  359.8 15.2 %collective-permute-start.21 = (f32[1,4,1,1024]{3,0,2,1:T(1,128)S(1)}, f32[1,4,1,1024]{3,0,2,1:T(1,128)S(1)}, u32[]{:S(2)}, u32[]{:S(2)}) collective-permute-start(f32[1,4,1,1024]{3,0,2,1:T(1,128)S(1)} %get-tuple-element.101), channel_id=1, source_target_pairs={{0,1},{1,2},{2,3},{3,4},{4,5},{5,6},{6,7},{8,9},{9,10},{10,11},{11... | collective-permute-start | bytes 49160 | tf_op jit(solution)/shard_map/ppermute | solution.py:21
  380.0 15.0 %collective-permute-start.23 = (f32[1,4,1,1024]{3,0,2,1:T(1,128)S(1)}, f32[1,4,1,1024]{3,0,2,1:T(1,128)S(1)}, u32[]{:S(2)}, u32[]{:S(2)}) collective-permute-start(f32[1,4,1,1024]{3,0,2,1:T(1,128)S(1)} %get-tuple-element.97), channel_id=1, source_target_pairs={{0,1},{1,2},{2,3},{3,4},{4,5},{5,6},{6,7},{8,9},{9,10},{10,11},{11... | collective-permute-start | bytes 49160 | tf_op jit(solution)/shard_map/ppermute | solution.py:21
  400.2 15.0 %collective-permute-start.25 = (f32[1,4,1,1024]{3,0,2,1:T(1,128)S(1)}, f32[1,4,1,1024]{3,0,2,1:T(1,128)S(1)}, u32[]{:S(2)}, u32[]{:S(2)}) collective-permute-start(f32[1,4,1,1024]{3,0,2,1:T(1,128)S(1)} %get-tuple-element.93), channel_id=1, source_target_pairs={{0,1},{1,2},{2,3},{3,4},{4,5},{5,6},{6,7},{8,9},{9,10},{10,11},{11... | collective-permute-start | bytes 49160 | tf_op jit(solution)/shard_map/ppermute | solution.py:21
  420.4 15.0 %collective-permute-start.27 = (f32[1,4,1,1024]{3,0,2,1:T(1,128)S(1)}, f32[1,4,1,1024]{3,0,2,1:T(1,128)S(1)}, u32[]{:S(2)}, u32[]{:S(2)}) collective-permute-start(f32[1,4,1,1024]{3,0,2,1:T(1,128)S(1)} %get-tuple-element.89), channel_id=1, source_target_pairs={{0,1},{1,2},{2,3},{3,4},{4,5},{5,6},{6,7},{8,9},{9,10},{10,11},{11... | collective-permute-start | bytes 49160 | tf_op jit(solution)/shard_map/ppermute | solution.py:21
  440.6 5.9 copy.46
  446.5 7.1 reshape.1693
  455.0 433.9 %reduce-scatter.4.cloned.1.call-done = f32[16,32]{1,0:T(8,128)} async-done(((f32[1024,32]{1,0:T(8,128)}), f32[16,32]{1,0:T(8,128)}) %reduce-scatter.4.cloned.1.call-update) | async-done | bytes 2064
  (133 shorter events, 65.0 us)
Async XLA Ops:
  7.2 881.8 %reduce-scatter.4.cloned.1.call-start = ((), (), s32[]{:S(2)}) async-start(), calls=%async_computation.1 | async-start | bytes 532480
  9.5 159.6 %collective-permute-start = (f32[1,4,1,1024]{3,0,2,1:T(1,128)S(1)}, f32[1,4,1,1024]{3,0,2,1:T(1,128)S(1)}, u32[]{:S(2)}, u32[]{:S(2)}) collective-permute-start(f32[1,4,1,1024]{3,0,2,1:T(1,128)S(1)} %get-tuple-element.140), channel_id=1, source_target_pairs={{1,0},{2,1},{3,2},{4,3},{5,4},{6,5},{7,6},{9,8},{10,9},{11,10},{12... | collective-permute-start | bytes 49160 | tf_op jit(solution)/shard_map/ppermute | solution.py:24
  12.1 156.9 %collective-permute-start.1 = (f32[1,4,1,1024]{3,0,2,1:T(1,128)S(1)}, f32[1,4,1,1024]{3,0,2,1:T(1,128)S(1)}, u32[]{:S(2)}, u32[]{:S(2)}) collective-permute-start(f32[1,4,1,1024]{3,0,2,1:T(1,128)S(1)} %get-tuple-element.141), channel_id=1, source_target_pairs={{0,1},{1,2},{2,3},{3,4},{4,5},{5,6},{6,7},{8,9},{9,10},{10,11},{11... | collective-permute-start | bytes 49160 | tf_op jit(solution)/shard_map/ppermute | solution.py:21
  160.3 27.3 %copy-start = (f32[8,16,1024]{2,0,1:T(8,128)}, f32[8,16,1024]{2,0,1:T(8,128)S(1)}, u32[]{:S(2)}) copy-start(f32[8,16,1024]{2,0,1:T(8,128)S(1)} %fusion.27) | copy-start | bytes 1572868
  163.2 24.5 %copy-start.1 = (f32[8,16,1024]{2,0,1:T(8,128)}, f32[8,16,1024]{2,0,1:T(8,128)S(1)}, u32[]{:S(2)}) copy-start(f32[8,16,1024]{2,0,1:T(8,128)S(1)} %fusion.24) | copy-start | bytes 1572868
  171.0 18.2 %collective-permute-start.2 = (f32[1,4,1,1024]{3,0,2,1:T(1,128)S(1)}, f32[1,4,1,1024]{3,0,2,1:T(1,128)S(1)}, u32[]{:S(2)}, u32[]{:S(2)}) collective-permute-start(f32[1,4,1,1024]{3,0,2,1:T(1,128)S(1)} %get-tuple-element.136), channel_id=1, source_target_pairs={{1,0},{2,1},{3,2},{4,3},{5,4},{6,5},{7,6},{9,8},{10,9},{11,10},{12... | collective-permute-start | bytes 49160 | tf_op jit(solution)/shard_map/ppermute | solution.py:24
  172.9 16.3 %collective-permute-start.3 = (f32[1,4,1,1024]{3,0,2,1:T(1,128)S(1)}, f32[1,4,1,1024]{3,0,2,1:T(1,128)S(1)}, u32[]{:S(2)}, u32[]{:S(2)}) collective-permute-start(f32[1,4,1,1024]{3,0,2,1:T(1,128)S(1)} %get-tuple-element.137), channel_id=1, source_target_pairs={{0,1},{1,2},{2,3},{3,4},{4,5},{5,6},{6,7},{8,9},{9,10},{10,11},{11... | collective-permute-start | bytes 49160 | tf_op jit(solution)/shard_map/ppermute | solution.py:21
  191.0 18.3 %collective-permute-start.4 = (f32[1,4,1,1024]{3,0,2,1:T(1,128)S(1)}, f32[1,4,1,1024]{3,0,2,1:T(1,128)S(1)}, u32[]{:S(2)}, u32[]{:S(2)}) collective-permute-start(f32[1,4,1,1024]{3,0,2,1:T(1,128)S(1)} %get-tuple-element.132), channel_id=1, source_target_pairs={{1,0},{2,1},{3,2},{4,3},{5,4},{6,5},{7,6},{9,8},{10,9},{11,10},{12... | collective-permute-start | bytes 49160 | tf_op jit(solution)/shard_map/ppermute | solution.py:24
  192.9 16.4 %collective-permute-start.5 = (f32[1,4,1,1024]{3,0,2,1:T(1,128)S(1)}, f32[1,4,1,1024]{3,0,2,1:T(1,128)S(1)}, u32[]{:S(2)}, u32[]{:S(2)}) collective-permute-start(f32[1,4,1,1024]{3,0,2,1:T(1,128)S(1)} %get-tuple-element.133), channel_id=1, source_target_pairs={{0,1},{1,2},{2,3},{3,4},{4,5},{5,6},{6,7},{8,9},{9,10},{10,11},{11... | collective-permute-start | bytes 49160 | tf_op jit(solution)/shard_map/ppermute | solution.py:21
  211.2 18.4 %collective-permute-start.6 = (f32[1,4,1,1024]{3,0,2,1:T(1,128)S(1)}, f32[1,4,1,1024]{3,0,2,1:T(1,128)S(1)}, u32[]{:S(2)}, u32[]{:S(2)}) collective-permute-start(f32[1,4,1,1024]{3,0,2,1:T(1,128)S(1)} %get-tuple-element.128), channel_id=1, source_target_pairs={{1,0},{2,1},{3,2},{4,3},{5,4},{6,5},{7,6},{9,8},{10,9},{11,10},{12... | collective-permute-start | bytes 49160 | tf_op jit(solution)/shard_map/ppermute | solution.py:24
  213.1 16.4 %collective-permute-start.7 = (f32[1,4,1,1024]{3,0,2,1:T(1,128)S(1)}, f32[1,4,1,1024]{3,0,2,1:T(1,128)S(1)}, u32[]{:S(2)}, u32[]{:S(2)}) collective-permute-start(f32[1,4,1,1024]{3,0,2,1:T(1,128)S(1)} %get-tuple-element.129), channel_id=1, source_target_pairs={{0,1},{1,2},{2,3},{3,4},{4,5},{5,6},{6,7},{8,9},{9,10},{10,11},{11... | collective-permute-start | bytes 49160 | tf_op jit(solution)/shard_map/ppermute | solution.py:21
  231.3 18.4 %collective-permute-start.8 = (f32[1,4,1,1024]{3,0,2,1:T(1,128)S(1)}, f32[1,4,1,1024]{3,0,2,1:T(1,128)S(1)}, u32[]{:S(2)}, u32[]{:S(2)}) collective-permute-start(f32[1,4,1,1024]{3,0,2,1:T(1,128)S(1)} %get-tuple-element.124), channel_id=1, source_target_pairs={{1,0},{2,1},{3,2},{4,3},{5,4},{6,5},{7,6},{9,8},{10,9},{11,10},{12... | collective-permute-start | bytes 49160 | tf_op jit(solution)/shard_map/ppermute | solution.py:24
  233.3 16.4 %collective-permute-start.9 = (f32[1,4,1,1024]{3,0,2,1:T(1,128)S(1)}, f32[1,4,1,1024]{3,0,2,1:T(1,128)S(1)}, u32[]{:S(2)}, u32[]{:S(2)}) collective-permute-start(f32[1,4,1,1024]{3,0,2,1:T(1,128)S(1)} %get-tuple-element.125), channel_id=1, source_target_pairs={{0,1},{1,2},{2,3},{3,4},{4,5},{5,6},{6,7},{8,9},{9,10},{10,11},{11... | collective-permute-start | bytes 49160 | tf_op jit(solution)/shard_map/ppermute | solution.py:21
  251.5 18.8 %collective-permute-start.10 = (f32[1,4,1,1024]{3,0,2,1:T(1,128)S(1)}, f32[1,4,1,1024]{3,0,2,1:T(1,128)S(1)}, u32[]{:S(2)}, u32[]{:S(2)}) collective-permute-start(f32[1,4,1,1024]{3,0,2,1:T(1,128)S(1)} %get-tuple-element.120), channel_id=1, source_target_pairs={{1,0},{2,1},{3,2},{4,3},{5,4},{6,5},{7,6},{9,8},{10,9},{11,10},{12... | collective-permute-start | bytes 49160 | tf_op jit(solution)/shard_map/ppermute | solution.py:24
  253.5 16.8 %collective-permute-start.11 = (f32[1,4,1,1024]{3,0,2,1:T(1,128)S(1)}, f32[1,4,1,1024]{3,0,2,1:T(1,128)S(1)}, u32[]{:S(2)}, u32[]{:S(2)}) collective-permute-start(f32[1,4,1,1024]{3,0,2,1:T(1,128)S(1)} %get-tuple-element.121), channel_id=1, source_target_pairs={{0,1},{1,2},{2,3},{3,4},{4,5},{5,6},{6,7},{8,9},{9,10},{10,11},{11... | collective-permute-start | bytes 49160 | tf_op jit(solution)/shard_map/ppermute | solution.py:21
  272.1 18.2 %collective-permute-start.12 = (f32[1,4,1,1024]{3,0,2,1:T(1,128)S(1)}, f32[1,4,1,1024]{3,0,2,1:T(1,128)S(1)}, u32[]{:S(2)}, u32[]{:S(2)}) collective-permute-start(f32[1,4,1,1024]{3,0,2,1:T(1,128)S(1)} %get-tuple-element.116), channel_id=1, source_target_pairs={{1,0},{2,1},{3,2},{4,3},{5,4},{6,5},{7,6},{9,8},{10,9},{11,10},{12... | collective-permute-start | bytes 49160 | tf_op jit(solution)/shard_map/ppermute | solution.py:24
  274.0 16.2 %collective-permute-start.13 = (f32[1,4,1,1024]{3,0,2,1:T(1,128)S(1)}, f32[1,4,1,1024]{3,0,2,1:T(1,128)S(1)}, u32[]{:S(2)}, u32[]{:S(2)}) collective-permute-start(f32[1,4,1,1024]{3,0,2,1:T(1,128)S(1)} %get-tuple-element.117), channel_id=1, source_target_pairs={{0,1},{1,2},{2,3},{3,4},{4,5},{5,6},{6,7},{8,9},{9,10},{10,11},{11... | collective-permute-start | bytes 49160 | tf_op jit(solution)/shard_map/ppermute | solution.py:21
  295.0 17.2 %collective-permute-start.14 = (f32[1,4,1,1024]{3,0,2,1:T(1,128)S(1)}, f32[1,4,1,1024]{3,0,2,1:T(1,128)S(1)}, u32[]{:S(2)}, u32[]{:S(2)}) collective-permute-start(f32[1,4,1,1024]{3,0,2,1:T(1,128)S(1)} %get-tuple-element.112), channel_id=1, source_target_pairs={{1,0},{2,1},{3,2},{4,3},{5,4},{6,5},{7,6},{9,8},{10,9},{11,10},{12... | collective-permute-start | bytes 49160 | tf_op jit(solution)/shard_map/ppermute | solution.py:24
  297.0 16.4 %collective-permute-start.15 = (f32[1,4,1,1024]{3,0,2,1:T(1,128)S(1)}, f32[1,4,1,1024]{3,0,2,1:T(1,128)S(1)}, u32[]{:S(2)}, u32[]{:S(2)}) collective-permute-start(f32[1,4,1,1024]{3,0,2,1:T(1,128)S(1)} %get-tuple-element.113), channel_id=1, source_target_pairs={{0,1},{1,2},{2,3},{3,4},{4,5},{5,6},{6,7},{8,9},{9,10},{10,11},{11... | collective-permute-start | bytes 49160 | tf_op jit(solution)/shard_map/ppermute | solution.py:21
  315.1 17.3 %collective-permute-start.16 = (f32[1,4,1,1024]{3,0,2,1:T(1,128)S(1)}, f32[1,4,1,1024]{3,0,2,1:T(1,128)S(1)}, u32[]{:S(2)}, u32[]{:S(2)}) collective-permute-start(f32[1,4,1,1024]{3,0,2,1:T(1,128)S(1)} %get-tuple-element.108), channel_id=1, source_target_pairs={{1,0},{2,1},{3,2},{4,3},{5,4},{6,5},{7,6},{9,8},{10,9},{11,10},{12... | collective-permute-start | bytes 49160 | tf_op jit(solution)/shard_map/ppermute | solution.py:24
  317.0 16.5 %collective-permute-start.17 = (f32[1,4,1,1024]{3,0,2,1:T(1,128)S(1)}, f32[1,4,1,1024]{3,0,2,1:T(1,128)S(1)}, u32[]{:S(2)}, u32[]{:S(2)}) collective-permute-start(f32[1,4,1,1024]{3,0,2,1:T(1,128)S(1)} %get-tuple-element.109), channel_id=1, source_target_pairs={{0,1},{1,2},{2,3},{3,4},{4,5},{5,6},{6,7},{8,9},{9,10},{10,11},{11... | collective-permute-start | bytes 49160 | tf_op jit(solution)/shard_map/ppermute | solution.py:21
  337.7 17.3 %collective-permute-start.18 = (f32[1,4,1,1024]{3,0,2,1:T(1,128)S(1)}, f32[1,4,1,1024]{3,0,2,1:T(1,128)S(1)}, u32[]{:S(2)}, u32[]{:S(2)}) collective-permute-start(f32[1,4,1,1024]{3,0,2,1:T(1,128)S(1)} %get-tuple-element.104), channel_id=1, source_target_pairs={{1,0},{2,1},{3,2},{4,3},{5,4},{6,5},{7,6},{9,8},{10,9},{11,10},{12... | collective-permute-start | bytes 49160 | tf_op jit(solution)/shard_map/ppermute | solution.py:24
  339.6 16.5 %collective-permute-start.19 = (f32[1,4,1,1024]{3,0,2,1:T(1,128)S(1)}, f32[1,4,1,1024]{3,0,2,1:T(1,128)S(1)}, u32[]{:S(2)}, u32[]{:S(2)}) collective-permute-start(f32[1,4,1,1024]{3,0,2,1:T(1,128)S(1)} %get-tuple-element.105), channel_id=1, source_target_pairs={{0,1},{1,2},{2,3},{3,4},{4,5},{5,6},{6,7},{8,9},{9,10},{10,11},{11... | collective-permute-start | bytes 49160 | tf_op jit(solution)/shard_map/ppermute | solution.py:21
  357.9 17.4 %collective-permute-start.20 = (f32[1,4,1,1024]{3,0,2,1:T(1,128)S(1)}, f32[1,4,1,1024]{3,0,2,1:T(1,128)S(1)}, u32[]{:S(2)}, u32[]{:S(2)}) collective-permute-start(f32[1,4,1,1024]{3,0,2,1:T(1,128)S(1)} %get-tuple-element.100), channel_id=1, source_target_pairs={{1,0},{2,1},{3,2},{4,3},{5,4},{6,5},{7,6},{9,8},{10,9},{11,10},{12... | collective-permute-start | bytes 49160 | tf_op jit(solution)/shard_map/ppermute | solution.py:24
  359.8 16.5 %collective-permute-start.21 = (f32[1,4,1,1024]{3,0,2,1:T(1,128)S(1)}, f32[1,4,1,1024]{3,0,2,1:T(1,128)S(1)}, u32[]{:S(2)}, u32[]{:S(2)}) collective-permute-start(f32[1,4,1,1024]{3,0,2,1:T(1,128)S(1)} %get-tuple-element.101), channel_id=1, source_target_pairs={{0,1},{1,2},{2,3},{3,4},{4,5},{5,6},{6,7},{8,9},{9,10},{10,11},{11... | collective-permute-start | bytes 49160 | tf_op jit(solution)/shard_map/ppermute | solution.py:21
  378.1 17.3 %collective-permute-start.22 = (f32[1,4,1,1024]{3,0,2,1:T(1,128)S(1)}, f32[1,4,1,1024]{3,0,2,1:T(1,128)S(1)}, u32[]{:S(2)}, u32[]{:S(2)}) collective-permute-start(f32[1,4,1,1024]{3,0,2,1:T(1,128)S(1)} %get-tuple-element.96), channel_id=1, source_target_pairs={{1,0},{2,1},{3,2},{4,3},{5,4},{6,5},{7,6},{9,8},{10,9},{11,10},{12... | collective-permute-start | bytes 49160 | tf_op jit(solution)/shard_map/ppermute | solution.py:24
  380.0 16.5 %collective-permute-start.23 = (f32[1,4,1,1024]{3,0,2,1:T(1,128)S(1)}, f32[1,4,1,1024]{3,0,2,1:T(1,128)S(1)}, u32[]{:S(2)}, u32[]{:S(2)}) collective-permute-start(f32[1,4,1,1024]{3,0,2,1:T(1,128)S(1)} %get-tuple-element.97), channel_id=1, source_target_pairs={{0,1},{1,2},{2,3},{3,4},{4,5},{5,6},{6,7},{8,9},{9,10},{10,11},{11... | collective-permute-start | bytes 49160 | tf_op jit(solution)/shard_map/ppermute | solution.py:21
  398.3 17.3 %collective-permute-start.24 = (f32[1,4,1,1024]{3,0,2,1:T(1,128)S(1)}, f32[1,4,1,1024]{3,0,2,1:T(1,128)S(1)}, u32[]{:S(2)}, u32[]{:S(2)}) collective-permute-start(f32[1,4,1,1024]{3,0,2,1:T(1,128)S(1)} %get-tuple-element.92), channel_id=1, source_target_pairs={{1,0},{2,1},{3,2},{4,3},{5,4},{6,5},{7,6},{9,8},{10,9},{11,10},{12... | collective-permute-start | bytes 49160 | tf_op jit(solution)/shard_map/ppermute | solution.py:24
  400.2 16.5 %collective-permute-start.25 = (f32[1,4,1,1024]{3,0,2,1:T(1,128)S(1)}, f32[1,4,1,1024]{3,0,2,1:T(1,128)S(1)}, u32[]{:S(2)}, u32[]{:S(2)}) collective-permute-start(f32[1,4,1,1024]{3,0,2,1:T(1,128)S(1)} %get-tuple-element.93), channel_id=1, source_target_pairs={{0,1},{1,2},{2,3},{3,4},{4,5},{5,6},{6,7},{8,9},{9,10},{10,11},{11... | collective-permute-start | bytes 49160 | tf_op jit(solution)/shard_map/ppermute | solution.py:21
  418.4 17.3 %collective-permute-start.26 = (f32[1,4,1,1024]{3,0,2,1:T(1,128)S(1)}, f32[1,4,1,1024]{3,0,2,1:T(1,128)S(1)}, u32[]{:S(2)}, u32[]{:S(2)}) collective-permute-start(f32[1,4,1,1024]{3,0,2,1:T(1,128)S(1)} %get-tuple-element.88), channel_id=1, source_target_pairs={{1,0},{2,1},{3,2},{4,3},{5,4},{6,5},{7,6},{9,8},{10,9},{11,10},{12... | collective-permute-start | bytes 49160 | tf_op jit(solution)/shard_map/ppermute | solution.py:24
  420.4 16.5 %collective-permute-start.27 = (f32[1,4,1,1024]{3,0,2,1:T(1,128)S(1)}, f32[1,4,1,1024]{3,0,2,1:T(1,128)S(1)}, u32[]{:S(2)}, u32[]{:S(2)}) collective-permute-start(f32[1,4,1,1024]{3,0,2,1:T(1,128)S(1)} %get-tuple-element.89), channel_id=1, source_target_pairs={{0,1},{1,2},{2,3},{3,4},{4,5},{5,6},{6,7},{8,9},{9,10},{10,11},{11... | collective-permute-start | bytes 49160 | tf_op jit(solution)/shard_map/ppermute | solution.py:21
Sparse Core Ops, SparseCore 0:
  453.7 435.1 reduce-scatter.3
where the time goes:
time: 901 us; the launch traced here: 898 us
  waiting for transfers between devices  442 us (49%)
  starting transfers between devices  237 us (26%)
  blocking collectives  128 us (14%)
  other arithmetic  34.9 us (4%)
  local copies, waits for them, and re-layouts  29 us (3%)
  between operations  15.8 us (2%)
  matrix products  11.2 us (1%)
    unnamed x2, waiting for transfers between devices  434 us
    ppermute x14, starting transfers between devices, extended(): lax.ppermute(lax.slice_in_dim(block, block.shape[dim] - width, None, axis...  210 us
    all_gather x1, blocking collectives, shards(): full_slow = lax.all_gather(slowness, 'freq', axis=2, tiled=True)  128 us
    ppermute x14, starting transfers between devices, extended(): lax.ppermute(lax.slice_in_dim(block, 0, width, axis=dim), axis, backward)  27.6 us
    unnamed x16, local copies, waits for them, and re-layouts  19.6 us
  transfers between devices with their start and end apart: 29, of which 8 were waited for; matrix products, arithmetic and copies ran while one was open for 3% of the time, Pallas kernels for 0%

commit v1 on v0

v1 whole, which is shorter than its diff:
```python
import math

import jax
import jax.numpy as jnp
import numpy as np
from jax import lax
from jax.experimental import pallas as pl
from jax.experimental.pallas import tpu as pltpu
from jax.sharding import PartitionSpec as P

MESH = pl.DeviceIdType.MESH
LANES, GROUP = 128, 16
ROWS, TOP, END, HALO = 48, 16, 32, 14
PEERS = 32
LAT = 8

COSINE = [0.9999983310699463, -0.499983549118042, 0.041640717536211014, -0.0013744860189035535, 2.1503588868654333e-05]
SINC = [0.9999998211860657, -0.16666515171527863, 0.008330939337611198, -0.00019708606123458594, 2.452983835610212e-06]


def polynomial(terms, t):
    value = jnp.float32(terms[-1]) * t + jnp.float32(terms[-2])
    for term in terms[-3::-1]:
        value = value * t + jnp.float32(term)
    return value


def node_phases(wavenum):
    half = 0.5 * (wavenum * wavenum)
    absorb = 0.1 * half
    absorb2 = absorb * absorb
    parts = []
    for j in range(8):
        excess = half - jnp.float32(0.5 * (math.pi * (j + 0.5) / 8) ** 2)
        square = excess * excess + absorb2
        modulus = square * lax.rsqrt(square)
        total = modulus + jnp.abs(excess)
        inverse = lax.rsqrt(total)
        larger, smaller = total * inverse, absorb * inverse
        propagating = excess >= 0
        kr = jnp.where(propagating, larger, smaller)
        ki = jnp.where(propagating, smaller, larger)
        attenuation = jnp.exp2(ki * jnp.float32(-1.4426950408889634))
        t = kr * kr
        parts.append((attenuation * polynomial(COSINE, t), (attenuation * kr) * polynomial(SINC, t)))
    return parts


def cosine_sums(p):
    def c(n, j):
        return float(np.float32((1.0 if n == 0 else 2.0) / 8 * math.cos(n * math.pi * (j + 0.5) / 8)))

    even = [p[j] + p[7 - j] for j in range(4)]
    odd = [p[j] - p[7 - j] for j in range(4)]
    s0, s1, d0, d1 = even[0] + even[3], even[1] + even[2], even[0] - even[3], even[1] - even[2]
    h = [None] * 8
    h[0] = (s0 + s1) * c(0, 0)
    h[4] = (s0 - s1) * c(4, 0)
    h[2] = d0 * c(2, 0) + d1 * c(2, 1)
    h[6] = d0 * c(6, 0) + d1 * c(6, 1)
    for n in (1, 3, 5, 7):
        h[n] = (odd[0] * c(n, 0) + odd[1] * c(n, 1)) + (odd[2] * c(n, 2) + odd[3] * c(n, 3))
    return h


def at_row(row):
    return pl.ds(pl.multiple_of(row * 8, 8), 8)


def kernel(
    freq_ref, slow_ref, src_ref, rec_ref, img_ref, src_out, rec_out,
    stage, T, D, H, packed, gathered, slow, share, partner_share, summed, blocks,
    in_sem, out_sem, own_send, own_recv, edge_send, edge_recv, halo_send, halo_recv,
    core_send, core_recv, pair_send, pair_recv, part_send, part_recv,
):
    f, l = lax.axis_index("freq"), lax.axis_index("lat")
    core, place = f % 2, f // 2
    z, x = place // 4, place % 4
    partner = (f + 1 - 2 * core, l)

    def peer(k):
        return lax.rem(place + k, PEERS)

    lane = lax.broadcasted_iota(jnp.int32, (8, LANES), 1)
    sub = lax.broadcasted_iota(jnp.int32, (8, LANES), 0)
    group = lane // GROUP
    first, last = lane == 0, lane == LANES - 1
    corner = ((sub == 0) & first) | ((sub == 7) & last)
    diagonal = sub == group

    barrier = pltpu.get_barrier_semaphore()

    def greet(device):
        pl.semaphore_signal(barrier, inc=1, device_id=device, device_id_type=MESH)

    def greet_all(k, carry):
        to = peer(k) * 2 + core

        @pl.when(l < LAT - 1)
        def _():
            greet((to, l + 1))

        @pl.when(l > 0)
        def _():
            greet((to, l - 1))

        return carry

    lax.fori_loop(0, PEERS, greet_all, 0)

    def greet_own(k, carry):
        greet((peer(k) * 2 + core, l))
        return carry

    lax.fori_loop(1, PEERS, greet_own, 0)
    greet(partner)

    fetches = [
        pltpu.make_async_copy(ref.at[0], stage.at[pl.ds(2 * i, 2)], in_sem.at[i])
        for i, ref in enumerate((src_ref, rec_ref))
    ]
    for copy in fetches:
        copy.start()

    for layer in range(2):
        for half in range(2):
            block = jnp.concatenate(
                [slow_ref[layer, 8 * half : 8 * half + 8, :], jnp.zeros((8, LANES - GROUP), jnp.float32)], axis=1
            )
            for turn in (16, 32, 64):
                block = block + pltpu.roll(block, turn, 1)
            row = jnp.sum(jnp.where(diagonal, block, 0.0), axis=0, keepdims=True)
            packed[2 * layer + half : 2 * layer + half + 1, :] = row

    for i, copy in enumerate(fetches):
        copy.wait()
        for c in (2 * i, 2 * i + 1):
            for t in range(2):
                for j in range(8):
                    T[0, c, pl.ds((TOP + 8 * t) * 8 + j, 8, stride=8), :] = stage[
                        c, 8 * t : 8 * t + 8, LANES * j : LANES * j + LANES
                    ]

    pl.semaphore_wait(barrier, PEERS + PEERS * jnp.where((l == 0) | (l == LAT - 1), 1, 2))

    def own_copy(k):
        return pltpu.make_async_remote_copy(
            src_ref=packed.at[pl.ds(0, 4)],
            dst_ref=gathered.at[core, x, pl.ds(0, 4), z],
            send_sem=own_send.at[k], recv_sem=own_recv.at[k],
            device_id=(peer(k) * 2 + core, l), device_id_type=MESH,
        )

    def edge_copy(k, side):
        return pltpu.make_async_remote_copy(
            src_ref=packed.at[1 - side],
            dst_ref=gathered.at[core, x, 4 + side, z],
            send_sem=edge_send.at[side, k], recv_sem=edge_recv.at[side, k],
            device_id=(peer(k) * 2 + core, l + 1 - 2 * side), device_id_type=MESH,
        )

    def halo_copy(pair, side):
        return pltpu.make_async_remote_copy(
            src_ref=T.at[0, pl.ds(2 * pair, 2), pl.ds((END - HALO if side == 0 else TOP) * 8, HALO * 8)],
            dst_ref=T.at[0, pl.ds(2 * pair, 2), pl.ds((TOP - HALO if side == 0 else END) * 8, HALO * 8)],
            send_sem=halo_send.at[side, pair], recv_sem=halo_recv.at[side, pair],
            device_id=(f, l + 1 - 2 * side), device_id_type=MESH,
        )

    def each(count, start, do):
        def body(k, carry):
            do(k)
            return carry

        lax.fori_loop(start, count, body, 0)

    sends = [l < LAT - 1, l > 0]
    receives = [l > 0, l < LAT - 1]

    def own_start(k):
        own_copy(k).start()

    each(PEERS, 1, own_start)
    for side in range(2):

        @pl.when(sends[side])
        def _(side=side):
            each(PEERS, 0, lambda k: edge_copy(k, side).start())

    for pair in range(2):
        for side in range(2):

            @pl.when(sends[side])
            def _(side=side, pair=pair):
                halo_copy(pair, side).start()

    for m in range(4):
        gathered[core, x, m, pl.ds(z, 1), :] = packed[m : m + 1, :]

    inside = [jnp.broadcast_to(l > 0, (1, 8, LANES)), jnp.broadcast_to(l < LAT - 1, (1, 8, LANES))]

    def clear_edges():
        for side, row in ((0, TOP - 1), (1, END)):

            @pl.when(jnp.logical_not(receives[side]))
            def _(row=row):
                for c in range(4):
                    T[0, c, pl.ds(row * 8, 8), :] = jnp.zeros((8, LANES), jnp.float32)

    clear_edges()

    each(PEERS, 1, lambda k: own_copy(k).wait_recv())
    for side in range(2):

        @pl.when(receives[side])
        def _(side=side):
            each(PEERS, 0, lambda k: edge_copy(k, side).wait_recv())

    core_copy = pltpu.make_async_remote_copy(
        src_ref=gathered.at[core], dst_ref=gathered.at[core], send_sem=core_send, recv_sem=core_recv,
        device_id=partner, device_id_type=MESH,
    )
    core_copy.start()
    core_copy.wait_recv()

    def swap_groups(v):
        v = list(v)
        for bit in (1, 2, 4):
            low = (group // bit) % 2 == 0
            for a in range(8):
                if not a & bit:
                    lo, hi = v[a], v[a + bit]
                    v[a] = jnp.where(low, lo, pltpu.roll(hi, GROUP * bit, 1))
                    v[a + bit] = jnp.where(low, pltpu.roll(lo, LANES - GROUP * bit, 1), hi)
        return v

    for m, to in ((0, 8), (1, 16), (4, 0), (5, 24), (2, 32), (3, 40)):
        rows = swap_groups([gathered[j % 2, j // 2, m] for j in range(8)])
        for g in range(8):
            slow[(to + g) * 8 : (to + g) * 8 + 8, :] = rows[g]

    frequency = freq_ref[0]

    def coefficients(start, count, unroll):
        def body(i, carry):
            for u in range(unroll):
                r = start + i * unroll + u
                parts = node_phases(slow[at_row(r), :] * frequency)
                for which in range(2):
                    for n, value in enumerate(cosine_sums([p[which] for p in parts])):
                        H[at_row(r * 16 + which * 8 + n), :] = value
            return carry

        lax.fori_loop(0, count // unroll, body, 0)

    coefficients(1, 30, 5)
    coefficients(32, 16, 4)

    def raise_rows(n, c, lo, hi, edge):
        B = hi - lo
        rows = pl.ds(lo * 8, B * 8)
        v = T[n - 1, c, pl.ds((lo - 1) * 8, (B + 2) * 8), :].reshape(B + 2, 8, LANES)
        e = v[:-1] + v[1:]
        q = e[:-1] + e[1:]
        stopped = jnp.where(corner[None], 0.0, q)
        left = pltpu.roll(jnp.where(last[None], pltpu.roll(stopped, 1, 1), q), 1, 2)
        right = pltpu.roll(jnp.where(first[None], pltpu.roll(stopped, 7, 1), q), LANES - 1, 2)
        s = (left + right) + (q + q)
        d = 0.125 * s if n == 1 else 0.25 * s - D[c, rows, :].reshape(B, 8, LANES)
        D[c, rows, :] = d.reshape(B * 8, LANES)
        value = d - v[1:-1]
        if edge is not None:
            parts = [value[:-1], jnp.where(inside[0], value[-1:], 0.0)] if edge == 0 else [jnp.where(inside[1], value[:1], 0.0), value[1:]]
            value = jnp.concatenate([part for part in parts if part.shape[0]], axis=0)
        T[n, c, rows, :] = value.reshape(B * 8, LANES)

    def levels(reach, pair):
        for n in range(1, 8):
            out = reach - n
            for lo, hi, edge in ((TOP - out, TOP, 0), (TOP, TOP + 8, None), (TOP + 8, END, None), (END, END + out, 1)):
                if lo < hi:
                    for c in range(2):
                        raise_rows(n, 2 * pair + c, lo, hi, edge)

    def accumulate(start, lo, count, unroll):
        def body(i, carry):
            for u in range(unroll):
                r = i * unroll + u
                total = [None] * 4
                for n in range(8):
                    hr = H[at_row((start + r) * 16 + n), :]
                    hi = H[at_row((start + r) * 16 + 8 + n), :]
                    t = [T[n, c, at_row(lo + r), :] for c in range(4)]
                    term = [
                        hr * t[0] - hi * t[1],
                        hr * t[1] + hi * t[0],
                        hr * t[2] + hi * t[3],
                        hr * t[3] - hi * t[2],
                    ]
                    total = term if n == 0 else [a + b for a, b in zip(total, term)]
                for c in range(4):
                    T[0, c, at_row(lo + r), :] = total[c]
            return carry

        lax.fori_loop(0, count // unroll, body, 0)

    def pair_copy(layer):
        return pltpu.make_async_remote_copy(
            src_ref=share.at[layer, 1 - core], dst_ref=partner_share.at[layer],
            send_sem=pair_send.at[layer], recv_sem=pair_recv.at[layer],
            device_id=partner, device_id_type=MESH,
        )

    def part_copy(layer, k):
        to = peer(k)
        return pltpu.make_async_remote_copy(
            src_ref=summed.at[layer, to % 4, :, to // 4], dst_ref=blocks.at[layer, place],
            send_sem=part_send.at[layer, k], recv_sem=part_recv.at[layer, k],
            device_id=(to * 2 + core, l), device_id_type=MESH,
        )

    def image_terms(layer):
        for m in range(2):
            terms = []
            for g in range(8):
                s_re, s_im, r_re, r_im = (T[0, c, pl.ds((TOP + 8 * m + g) * 8, 8), :] for c in range(4))
                terms.append(s_re * r_re + s_im * r_im)
            for j, value in enumerate(swap_groups(terms)):
                share[layer, j % 2, j // 2, m] = value
        pair_copy(layer).start()

    def image_parts(layer):
        pair_copy(layer).wait_recv()
        summed[layer] = share[layer, core] + partner_share[layer]
        each(PEERS, 1, lambda k: part_copy(layer, k).start())
        for m in range(2):
            blocks[layer, place, m : m + 1, :] = summed[layer, x, m, pl.ds(z, 1), :]

    def image_sum(layer):
        each(PEERS, 1, lambda k: part_copy(layer, k).wait_recv())
        total = jnp.sum(blocks[layer], axis=0) * 0.125
        for m in range(2):
            row = jnp.where(diagonal, jnp.broadcast_to(total[m : m + 1, :], (8, LANES)), 0.0)
            for turn in (64, 32, 16):
                row = row + pltpu.roll(row, turn, 1)
            img_ref[layer, 8 * m : 8 * m + 8, :] = row[:, :GROUP]

    def first_levels(pair, carry):
        for side in range(2):

            @pl.when(receives[side])
            def _(side=side):
                halo_copy(pair, side).wait_recv()

        levels(HALO, pair)
        return carry

    lax.fori_loop(0, 2, first_levels, 0)
    for pair in range(2):
        for side in range(2):

            @pl.when(sends[side])
            def _(side=side, pair=pair):
                halo_copy(pair, side).wait_send()

    accumulate(1, TOP - 7, 30, 5)
    clear_edges()
    image_terms(0)

    levels(HALO // 2, 0)
    image_parts(0)
    levels(HALO // 2, 1)
    accumulate(32, TOP, 16, 4)
    image_terms(1)
    for c in range(4):
        for t in range(2):
            for j in range(8):
                stage[c, 8 * t : 8 * t + 8, LANES * j : LANES * j + LANES] = T[
                    0, c, pl.ds((TOP + 8 * t) * 8 + j, 8, stride=8), :
                ]
    stores = [
        pltpu.make_async_copy(stage.at[pl.ds(2 * i, 2)], ref.at[0], out_sem.at[i])
        for i, ref in enumerate((src_out, rec_out))
    ]
    image_parts(1)
    for copy in stores:
        copy.start()
    image_sum(0)
    each(PEERS, 1, lambda k: own_copy(k).wait_send())
    for side in range(2):

        @pl.when(sends[side])
        def _(side=side):
            each(PEERS, 0, lambda k: edge_copy(k, side).wait_send())

    core_copy.wait_send()
    for layer in range(2):
        pair_copy(layer).wait_send()
        each(PEERS, 1, lambda k: part_copy(layer, k).wait_send())
    for copy in stores:
        copy.wait()
    image_sum(1)


def migrate(frequencies, slowness, src_field, rec_field):
    f32 = jnp.float32
    field = jax.ShapeDtypeStruct(src_field.shape, f32)
    dma = pltpu.SemaphoreType.DMA
    return pl.pallas_call(
        kernel,
        out_shape=(jax.ShapeDtypeStruct(slowness.shape, f32), field, field),
        in_specs=[
            pl.BlockSpec(memory_space=pltpu.SMEM),
            pl.BlockSpec(memory_space=pltpu.VMEM),
            pl.BlockSpec(memory_space=pltpu.HBM),
            pl.BlockSpec(memory_space=pltpu.HBM),
        ],
        out_specs=(
            pl.BlockSpec(memory_space=pltpu.VMEM),
            pl.BlockSpec(memory_space=pl.ANY),
            pl.BlockSpec(memory_space=pl.ANY),
        ),
        scratch_shapes=[
            pltpu.VMEM((4, 16, 1024), f32),
            pltpu.VMEM((8, 4, ROWS * 8, LANES), f32),
            pltpu.VMEM((4, ROWS * 8, LANES), f32),
            pltpu.VMEM((48 * 16 * 8, LANES), f32),
            pltpu.VMEM((4, LANES), f32),
            pltpu.VMEM((2, 4, 6, 8, LANES), f32),
            pltpu.VMEM((48 * 8, LANES), f32),
            pltpu.VMEM((2, 2, 4, 2, 8, LANES), f32),
            pltpu.VMEM((2, 4, 2, 8, LANES), f32),
            pltpu.VMEM((2, 4, 2, 8, LANES), f32),
            pltpu.VMEM((2, PEERS, 2, LANES), f32),
            dma((2,)), dma((2,)),
            dma((PEERS,)), dma((PEERS,)),
            dma((2, PEERS)), dma((2, PEERS)),
            dma((2, 2)), dma((2, 2)),
            dma, dma,
            dma((2,)), dma((2,)),
            dma((2, PEERS)), dma((2, PEERS)),
        ],
        compiler_params=pltpu.CompilerParams(collective_id=0, has_side_effects=True, vmem_limit_bytes=40 << 20),
        name="migrate",
    )(frequencies, slowness, src_field, rec_field)


def solution(mesh):
    fields = P("freq", None, "lat", None)
    return jax.shard_map(
        migrate,
        mesh=mesh,
        in_specs=(P("freq"), P(None, "lat", "freq"), fields, fields),
        out_specs=(P(None, "lat", "freq"), fields, fields),
        check_vma=False,
    )
```

time: 901 us -> 67.3 us (0.07)
  waiting for transfers between devices: 442 us -> 0 us
  starting transfers between devices: 237 us -> 0 us
  blocking collectives: 128 us -> 0 us
  Pallas kernels: 0 us -> 61.4 us
  other arithmetic: 34.9 us -> 0 us
  local copies, waits for them, and re-layouts: 29 us -> 4.44 us
  between operations: 15.8 us -> 1.3 us
  matrix products: 11.2 us -> 0 us
    unnamed x2 -> x0, waiting for transfers between devices: 434 us -> none
    ppermute x28 -> x0, starting transfers between devices: 237 us -> none  [the longest x14 210 us: extended(): lax.ppermute(lax.slice_in_dim(block, block.shape[dim] - width, None, axis...]
    all_gather x1 -> x0, blocking collectives: 128 us -> none  [shards(): full_slow = lax.all_gather(slowness, 'freq', axis=2, tiled=True)]
    pallas_call x0 -> x1, Pallas kernels: none -> 61.4 us  [migrate(): pl.pallas_call(kernel, out_shape=(jax.ShapeDtypeStruct(slowness.shape, f3...]
    unnamed x16 -> x9, local copies, waits for them, and re-layouts: 19.6 us -> 4.44 us
    another operation x17 -> x0, other arithmetic: 12.9 us -> none  [the longest x16 12.7 us: accumulate(): jnp.stack([coef_re * src_re - coef_im * src_im, coef_re * src_im + coef_i...]
    sub x12 -> x0, other arithmetic: 12.2 us -> none  [rim_step(): following = 2.0 * raise_level(current) - previous]
    dot_general x4 -> x0, matrix products: 11.2 us -> none  [the longest x2 5.6 us: coefficients(): jnp.einsum('nj,j...->n...', cosine_table, phase_im, precision=lax.Precisi...]
  transfers between devices with their start and end apart: 29 -> 0, of which waited for: 8 -> 0; matrix products, arithmetic and copies ran while one was open for 3% -> 0% of each run, Pallas kernels for 0% -> 0%
where the time goes in v1:
time: 67.3 us; the launch traced here: 67.1 us
  Pallas kernels  61.4 us (91%)
  local copies, waits for them, and re-layouts  4.44 us (7%)
  between operations  1.3 us (2%)
    pallas_call x1, Pallas kernels, migrate(): pl.pallas_call(kernel, out_shape=(jax.ShapeDtypeStruct(slowness.shape, f3...  61.4 us
    unnamed x9, local copies, waits for them, and re-layouts  4.44 us

profile of v1, /device:TPU:24, one launch (start us, length us, event | category | flops | bytes accessed | tf_op | source)
XLA Modules:
  0.0 67.1 jit_solution(18239307952625724826)
XLA Ops:
  1.3 0.0 copy-start
  1.3 0.9 %copy-done = f32[1,2,16,1024]{3,2,1,0:T(8,128)S(1)} copy-done((f32[1,2,16,1024]{3,2,1,0:T(8,128)S(1)}, f32[1,2,16,1024]{3,2,1,0:T(8,128)}, u32[]{:S(2)}) %copy-start) | copy-done | bytes 131096
  2.2 0.0 copy-start.1
  2.2 0.9 %copy-done.1 = f32[1,2,16,1024]{3,2,1,0:T(8,128)S(1)} copy-done((f32[1,2,16,1024]{3,2,1,0:T(8,128)S(1)}, f32[1,2,16,1024]{3,2,1,0:T(8,128)}, u32[]{:S(2)}) %copy-start.1) | copy-done | bytes 131096
  3.1 0.0 copy-start.2
  3.1 0.7 %copy-done.2 = f32[2,16,16]{2,1,0:T(8,128)S(1)} copy-done((f32[2,16,16]{2,1,0:T(8,128)S(1)}, f32[2,16,16]{2,1,0:T(8,128)}, u32[]{:S(2)}) %copy-start.2) | copy-done | bytes 2072
  3.8 61.4 %migrate.1 = (f32[2,16,16]{2,1,0:T(8,128)S(1)}, f32[1,2,16,1024]{3,2,1,0:T(8,128)S(1)}, f32[1,2,16,1024]{3,2,1,0:T(8,128)S(1)}) custom-call(f32[1]{0:T(128)S(6)} %copy.10.freq_ref, f32[2,16,16]{2,1,0:T(8,128)S(1)} %copy-done.2, f32[1,2,16,1024]{3,2,1,0:T(8,128)S(1)} %copy-done, f32[1,2,16,1024]{3,2,1,0:T(8,128)S(1)} %copy-done.1), custom_call_target="tpu_custom_call" | custom-call | tf_op jit(solution)/shard_map/migrate/pallas_call | solution.py:409
  65.2 0.6 copy.11
  65.8 0.7 copy.12
  66.4 0.7 copy.13
Async XLA Ops:
  1.3 0.9 %copy-start = (f32[1,2,16,1024]{3,2,1,0:T(8,128)S(1)}, f32[1,2,16,1024]{3,2,1,0:T(8,128)}, u32[]{:S(2)}) copy-start(f32[1,2,16,1024]{3,2,1,0:T(8,128)} %src_ref.1) | copy-start | bytes 393220
  2.2 0.9 %copy-start.1 = (f32[1,2,16,1024]{3,2,1,0:T(8,128)S(1)}, f32[1,2,16,1024]{3,2,1,0:T(8,128)}, u32[]{:S(2)}) copy-start(f32[1,2,16,1024]{3,2,1,0:T(8,128)} %rec_ref.1) | copy-start | bytes 393220
  3.1 0.7 %copy-start.2 = (f32[2,16,16]{2,1,0:T(8,128)S(1)}, f32[2,16,16]{2,1,0:T(8,128)}, u32[]{:S(2)}) copy-start(f32[2,16,16]{2,1,0:T(8,128)} %slow_ref.1) | copy-start | bytes 6148

commit v2 on v1

--- a/solution.py
+++ b/solution.py
@@ -68,9 +68,9 @@
 
 
 def kernel(
-    freq_ref, slow_ref, src_ref, rec_ref, img_ref, src_out, rec_out,
-    stage, T, D, H, packed, gathered, slow, share, partner_share, summed, blocks,
-    in_sem, out_sem, own_send, own_recv, edge_send, edge_recv, halo_send, halo_recv,
+    freq_hbm, slow_hbm, src_ref, rec_ref, img_ref, src_out, rec_out,
+    freq_ref, slow_ref, stage, T, D, H, packed, gathered, slow, relay, share, partner_share, summed, blocks,
+    in_sem, out_sem, own_send, own_recv, edge_send, edge_recv, halo_send, halo_recv, relay_send, relay_recv,
     core_send, core_recv, pair_send, pair_recv, part_send, part_recv,
 ):
     f, l = lax.axis_index("freq"), lax.axis_index("lat")
@@ -88,39 +88,50 @@
     corner = ((sub == 0) & first) | ((sub == 7) & last)
     diagonal = sub == group
 
-    barrier = pltpu.get_barrier_semaphore()
-
-    def greet(device):
-        pl.semaphore_signal(barrier, inc=1, device_id=device, device_id_type=MESH)
-
-    def greet_all(k, carry):
-        to = peer(k) * 2 + core
-
-        @pl.when(l < LAT - 1)
-        def _():
-            greet((to, l + 1))
-
-        @pl.when(l > 0)
-        def _():
-            greet((to, l - 1))
-
-        return carry
-
-    lax.fori_loop(0, PEERS, greet_all, 0)
-
-    def greet_own(k, carry):
-        greet((peer(k) * 2 + core, l))
-        return carry
-
-    lax.fori_loop(1, PEERS, greet_own, 0)
-    greet(partner)
-
     fetches = [
         pltpu.make_async_copy(ref.at[0], stage.at[pl.ds(2 * i, 2)], in_sem.at[i])
         for i, ref in enumerate((src_ref, rec_ref))
     ]
-    for copy in fetches:
+    fetch_slow = pltpu.make_async_copy(slow_hbm, slow_ref, in_sem.at[2])
+    fetch_freq = pltpu.make_async_copy(freq_hbm, freq_ref, in_sem.at[3])
+    for copy in (fetch_slow, *fetches, fetch_freq):
         copy.start()
+
+    barrier = pltpu.get_barrier_semaphore()
+
+    def greet(device):
+        pl.semaphore_signal(barrier, inc=1, device_id=device, device_id_type=MESH)
+
+    for k in range(PEERS - 1, -1, -1):
+        to = peer(k) * 2 + core
+
+        @pl.when(l < LAT - 1)
+        def _(to=to):
+            greet((to, l + 1))
+
+        @pl.when(l > 0)
+        def _(to=to):
+            greet((to, l - 1))
+
+    for k in range(PEERS - 1, 0, -1):
+        greet((peer(k) * 2 + core, l))
+    for k in range(2, LAT - 1):
+        away = lax.rem(l + k, LAT)
+
+        @pl.when((away - l) * (away - l) > 1)
+        def _(away=away):
+            greet((f, away))
+
+    for k in (1, LAT - 1):
+        away = lax.rem(l + k, LAT)
+
+        @pl.when((away - l) * (away - l) > 1)
+        def _(away=away):
+            greet((f, away))
+
+    greet(partner)
+
+    fetch_slow.wait()
 
     for layer in range(2):
         for half in range(2):
@@ -141,13 +152,13 @@
                         c, 8 * t : 8 * t + 8, LANES * j : LANES * j + LANES
                     ]
 
-    pl.semaphore_wait(barrier, PEERS + PEERS * jnp.where((l == 0) | (l == LAT - 1), 1, 2))
+    pl.semaphore_wait(barrier, PEERS + jnp.where((l == 0) | (l == LAT - 1), PEERS + LAT - 2, 2 * PEERS + LAT - 3))
 
     def own_copy(k):
         return pltpu.make_async_remote_copy(
             src_ref=packed.at[pl.ds(0, 4)],
             dst_ref=gathered.at[core, x, pl.ds(0, 4), z],
-            send_sem=own_send.at[k], recv_sem=own_recv.at[k],
+            send_sem=own_send, recv_sem=own_recv,
             device_id=(peer(k) * 2 + core, l), device_id_type=MESH,
         )
 
@@ -155,44 +166,73 @@
         return pltpu.make_async_remote_copy(
             src_ref=packed.at[1 - side],
             dst_ref=gathered.at[core, x, 4 + side, z],
-            send_sem=edge_send.at[side, k], recv_sem=edge_recv.at[side, k],
+            send_sem=edge_send.at[side], recv_sem=edge_recv.at[side],
             device_id=(peer(k) * 2 + core, l + 1 - 2 * side), device_id_type=MESH,
         )
 
-    def halo_copy(pair, side):
-        return pltpu.make_async_remote_copy(
-            src_ref=T.at[0, pl.ds(2 * pair, 2), pl.ds((END - HALO if side == 0 else TOP) * 8, HALO * 8)],
-            dst_ref=T.at[0, pl.ds(2 * pair, 2), pl.ds((TOP - HALO if side == 0 else END) * 8, HALO * 8)],
-            send_sem=halo_send.at[side, pair], recv_sem=halo_recv.at[side, pair],
+    def halo_rows(side):
+        down = side == 0
+        return (END - HALO, TOP - HALO) if down else (TOP, END)
+
+    def halo_copy(c, side):
+        read, land = halo_rows(side)
+        return pltpu.make_async_remote_copy(
+            src_ref=T.at[0, c, pl.ds(read * 8, HALO * 8)],
+            dst_ref=T.at[0, c, pl.ds(land * 8, HALO * 8)],
+            send_sem=halo_send.at[side, c], recv_sem=halo_recv.at[side, c],
             device_id=(f, l + 1 - 2 * side), device_id_type=MESH,
         )
 
-    def each(count, start, do):
-        def body(k, carry):
-            do(k)
-            return carry
-
-        lax.fori_loop(start, count, body, 0)
+    lower = l < LAT // 2
+    step = jnp.where(lower, l, LAT - 1 - l)
+    across = jnp.where(lower, LAT // 2, LAT // 2 - 1)
+
+    def to_relay(c, side):
+        read, _ = halo_rows(side)
+        return pltpu.make_async_remote_copy(
+            src_ref=T.at[0, c, pl.ds(read * 8, HALO * 8)], dst_ref=relay,
+            send_sem=relay_send.at[c], recv_sem=relay_recv.at[0],
+            device_id=(f, c if side == 0 else LAT - 1 - c), device_id_type=MESH,
+        )
+
+    def from_relay(c, side):
+        _, land = halo_rows(side)
+        return pltpu.make_async_remote_copy(
+            src_ref=relay, dst_ref=T.at[0, c, pl.ds(land * 8, HALO * 8)],
+            send_sem=relay_send.at[3], recv_sem=halo_recv.at[side, c],
+            device_id=(f, across), device_id_type=MESH,
+        )
+
+    def bytes_of(rows, sem):
+        return pltpu.make_async_copy(H.at[pl.ds(0, rows)], H.at[pl.ds(0, rows)], sem)
 
     sends = [l < LAT - 1, l > 0]
     receives = [l > 0, l < LAT - 1]
 
-    def own_start(k):
+    middle = [l == LAT // 2 - 1, l == LAT // 2]
+    for side in range(2):
+
+        @pl.when(middle[side])
+        def _(side=side):
+            for c in range(3):
+                to_relay(c, side).start()
+            halo_copy(3, side).start()
+
+    for k in range(PEERS - 1, 0, -1):
         own_copy(k).start()
-
-    each(PEERS, 1, own_start)
     for side in range(2):
 
         @pl.when(sends[side])
         def _(side=side):
-            each(PEERS, 0, lambda k: edge_copy(k, side).start())
-
-    for pair in range(2):
-        for side in range(2):
-
-            @pl.when(sends[side])
-            def _(side=side, pair=pair):
-                halo_copy(pair, side).start()
+            for k in range(PEERS - 1, -1, -1):
+                edge_copy(k, side).start()
+
+    for side in range(2):
+
+        @pl.when(sends[side] & jnp.logical_not(middle[side]))
+        def _(side=side):
+            for c in range(4):
+                halo_copy(c, side).start()
 
     for m in range(4):
         gathered[core, x, m, pl.ds(z, 1), :] = packed[m : m + 1, :]
@@ -209,12 +249,20 @@
 
     clear_edges()
 
-    each(PEERS, 1, lambda k: own_copy(k).wait_recv())
+    for c in range(3):
+        for side in range(2):
+
+            @pl.when((step == c) & (lower if side == 0 else jnp.logical_not(lower)))
+            def _(c=c, side=side):
+                to_relay(c, side).wait_recv()
+                from_relay(c, side).start()
+
+    bytes_of(4 * (PEERS - 1), own_recv).wait()
     for side in range(2):
 
         @pl.when(receives[side])
         def _(side=side):
-            each(PEERS, 0, lambda k: edge_copy(k, side).wait_recv())
+            bytes_of(PEERS, edge_recv.at[side]).wait()
 
     core_copy = pltpu.make_async_remote_copy(
         src_ref=gathered.at[core], dst_ref=gathered.at[core], send_sem=core_send, recv_sem=core_recv,
@@ -239,6 +287,7 @@
         for g in range(8):
             slow[(to + g) * 8 : (to + g) * 8 + 8, :] = rows[g]
 
+    fetch_freq.wait()
     frequency = freq_ref[0]
 
     def coefficients(start, count, unroll):
@@ -315,7 +364,7 @@
         to = peer(k)
         return pltpu.make_async_remote_copy(
             src_ref=summed.at[layer, to % 4, :, to // 4], dst_ref=blocks.at[layer, place],
-            send_sem=part_send.at[layer, k], recv_sem=part_recv.at[layer, k],
+            send_sem=part_send.at[layer], recv_sem=part_recv.at[layer],
             device_id=(to * 2 + core, l), device_id_type=MESH,
         )
 
@@ -332,12 +381,13 @@
     def image_parts(layer):
         pair_copy(layer).wait_recv()
         summed[layer] = share[layer, core] + partner_share[layer]
-        each(PEERS, 1, lambda k: part_copy(layer, k).start())
+        for k in range(PEERS - 1, 0, -1):
+            part_copy(layer, k).start()
         for m in range(2):
             blocks[layer, place, m : m + 1, :] = summed[layer, x, m, pl.ds(z, 1), :]
 
     def image_sum(layer):
-        each(PEERS, 1, lambda k: part_copy(layer, k).wait_recv())
+        bytes_of(2 * (PEERS - 1), part_recv.at[layer]).wait()
         total = jnp.sum(blocks[layer], axis=0) * 0.125
         for m in range(2):
             row = jnp.where(diagonal, jnp.broadcast_to(total[m : m + 1, :], (8, LANES)), 0.0)
@@ -350,18 +400,29 @@
 
             @pl.when(receives[side])
             def _(side=side):
-                halo_copy(pair, side).wait_recv()
+                for c in range(2):
+                    halo_copy(2 * pair + c, side).wait_recv()
 
         levels(HALO, pair)
         return carry
 
     lax.fori_loop(0, 2, first_levels, 0)
-    for pair in range(2):
-        for side in range(2):
-
-            @pl.when(sends[side])
-            def _(side=side, pair=pair):
-                halo_copy(pair, side).wait_send()
+    for side in range(2):
+
+        @pl.when(sends[side] & jnp.logical_not(middle[side]))
+        def _(side=side):
+            for c in range(4):
+                halo_copy(c, side).wait_send()
+
+        @pl.when(middle[side])
+        def _(side=side):
+            for c in range(3):
+                to_relay(c, side).wait_send()
+            halo_copy(3, side).wait_send()
+
+    @pl.when(step < 3)
+    def _():
+        from_relay(0, 0).wait_send()
 
     accumulate(1, TOP - 7, 30, 5)
     clear_edges()
@@ -386,17 +447,17 @@
     for copy in stores:
         copy.start()
     image_sum(0)
-    each(PEERS, 1, lambda k: own_copy(k).wait_send())
+    bytes_of(4 * (PEERS - 1), own_send).wait()
     for side in range(2):
 
         @pl.when(sends[side])
         def _(side=side):
-            each(PEERS, 0, lambda k: edge_copy(k, side).wait_send())
+            bytes_of(PEERS, edge_send.at[side]).wait()
 
     core_copy.wait_send()
     for layer in range(2):
         pair_copy(layer).wait_send()
-        each(PEERS, 1, lambda k: part_copy(layer, k).wait_send())
+        bytes_of(2 * (PEERS - 1), part_send.at[layer]).wait()
     for copy in stores:
         copy.wait()
     image_sum(1)
@@ -410,8 +471,8 @@
         kernel,
         out_shape=(jax.ShapeDtypeStruct(slowness.shape, f32), field, field),
         in_specs=[
-            pl.BlockSpec(memory_space=pltpu.SMEM),
-            pl.BlockSpec(memory_space=pltpu.VMEM),
+            pl.BlockSpec(memory_space=pltpu.HBM),
+            pl.BlockSpec(memory_space=pltpu.HBM),
             pl.BlockSpec(memory_space=pltpu.HBM),
             pl.BlockSpec(memory_space=pltpu.HBM),
         ],
@@ -421,6 +482,8 @@
             pl.BlockSpec(memory_space=pl.ANY),
         ),
         scratch_shapes=[
+            pltpu.SMEM((1,), f32),
+            pltpu.VMEM((2, 16, 16), f32),
             pltpu.VMEM((4, 16, 1024), f32),
             pltpu.VMEM((8, 4, ROWS * 8, LANES), f32),
             pltpu.VMEM((4, ROWS * 8, LANES), f32),
@@ -428,19 +491,21 @@
             pltpu.VMEM((4, LANES), f32),
             pltpu.VMEM((2, 4, 6, 8, LANES), f32),
             pltpu.VMEM((48 * 8, LANES), f32),
+            pltpu.VMEM((HALO * 8, LANES), f32),
             pltpu.VMEM((2, 2, 4, 2, 8, LANES), f32),
             pltpu.VMEM((2, 4, 2, 8, LANES), f32),
             pltpu.VMEM((2, 4, 2, 8, LANES), f32),
             pltpu.VMEM((2, PEERS, 2, LANES), f32),
-            dma((2,)), dma((2,)),
-            dma((PEERS,)), dma((PEERS,)),
-            dma((2, PEERS)), dma((2, PEERS)),
-            dma((2, 2)), dma((2, 2)),
+            dma((4,)), dma((2,)),
             dma, dma,
             dma((2,)), dma((2,)),
-            dma((2, PEERS)), dma((2, PEERS)),
+            dma((2, 4)), dma((2, 4)),
+            dma((4,)), dma((4,)),
+            dma, dma,
+            dma((2,)), dma((2,)),
+            dma((2,)), dma((2,)),
         ],
-        compiler_params=pltpu.CompilerParams(collective_id=0, has_side_effects=True, vmem_limit_bytes=40 << 20),
+        compiler_params=pltpu.CompilerParams(collective_id=0, has_side_effects=True, vmem_limit_bytes=64 << 20),
         name="migrate",
     )(frequencies, slowness, src_field, rec_field)
 

time: 67.3 us -> 56.5 us (0.84)
  the two profiles are of different devices: /device:TPU:24 before, /device:TPU:8 now
where the time goes in v2:
time: 56.5 us; the launch traced here: 56.3 us
  Pallas kernels  51.4 us (91%)
  local copies, waits for them, and re-layouts  3.59 us (6%)
  between operations  1.29 us (2%)
    pallas_call x1, Pallas kernels, migrate(): pl.pallas_call(kernel, out_shape=(jax.ShapeDtypeStruct(slowness.shape, f3...  51.4 us
    unnamed x5, local copies, waits for them, and re-layouts  3.59 us

profile of v2, /device:TPU:8, one launch (start us, length us, event | category | flops | bytes accessed | tf_op | source)
XLA Modules:
  0.0 56.3 jit_solution(10325544569757217705)
XLA Ops:
  1.3 51.4 %migrate.1 = (f32[2,16,16]{2,1,0:T(8,128)}, f32[1,2,16,1024]{3,2,1,0:T(8,128)}, f32[1,2,16,1024]{3,2,1,0:T(8,128)}) custom-call(f32[1]{0:T(128)S(6)} %copy.10.freq_hbm, f32[2,16,16]{2,1,0:T(8,128)} %slow_hbm.1, f32[1,2,16,1024]{3,2,1,0:T(8,128)} %src_ref.1, f32[1,2,16,1024]{3,2,1,0:T(8,128)} %rec_ref.1), custom_call_target="tpu_custom_call" | custom-call | tf_op jit(solution)/shard_map/migrate/pallas_call | solution.py:470
  52.7 1.3 %copy.11 = f32[2,16,16]{2,1,0:T(8,128)} copy(f32[2,16,16]{2,1,0:T(8,128)} %get-tuple-element.6) | data formatting | bytes 4096
  54.0 0.0 copy-start
  54.0 1.6 %copy.12 = f32[1,2,16,1024]{3,2,1,0:T(8,128)} copy(f32[1,2,16,1024]{3,2,1,0:T(8,128)} %get-tuple-element.7) | data formatting | bytes 262144
  55.6 0.0 copy-done
  55.6 0.7 %copy.13 = f32[1,2,16,1024]{3,2,1,0:T(8,128)} copy(f32[1,2,16,1024]{3,2,1,0:T(8,128)S(1)} %copy-done) | data formatting | bytes 262144
Async XLA Ops:
  54.0 1.6 %copy-start = (f32[1,2,16,1024]{3,2,1,0:T(8,128)S(1)}, f32[1,2,16,1024]{3,2,1,0:T(8,128)}, u32[]{:S(2)}) copy-start(f32[1,2,16,1024]{3,2,1,0:T(8,128)} %get-tuple-element.8) | copy-start | bytes 393220

commit v3 on v2

--- a/solution.py
+++ b/solution.py
@@ -102,32 +102,28 @@
     def greet(device):
         pl.semaphore_signal(barrier, inc=1, device_id=device, device_id_type=MESH)
 
-    for k in range(PEERS - 1, -1, -1):
-        to = peer(k) * 2 + core
+    for to in range(PEERS):
+
+        @pl.when(to != place)
+        def _(to=to):
+            greet((to * 2 + core, l))
+
+    for to in range(PEERS):
 
         @pl.when(l < LAT - 1)
         def _(to=to):
-            greet((to, l + 1))
+            greet((to * 2 + core, l + 1))
 
         @pl.when(l > 0)
         def _(to=to):
-            greet((to, l - 1))
-
-    for k in range(PEERS - 1, 0, -1):
-        greet((peer(k) * 2 + core, l))
-    for k in range(2, LAT - 1):
-        away = lax.rem(l + k, LAT)
-
-        @pl.when((away - l) * (away - l) > 1)
-        def _(away=away):
-            greet((f, away))
-
-    for k in (1, LAT - 1):
-        away = lax.rem(l + k, LAT)
-
-        @pl.when((away - l) * (away - l) > 1)
-        def _(away=away):
-            greet((f, away))
+            greet((to * 2 + core, l - 1))
+
+    for one, other in ((3, 0), (3, 1), (4, 0), (4, 1), (4, 2), (3, 5), (3, 6), (3, 7), (4, 6), (4, 7)):
+        for here, there in ((one, other), (other, one)):
+
+            @pl.when(l == here)
+            def _(there=there):
+                greet((f, there))
 
     greet(partner)
 
@@ -152,7 +148,8 @@
                         c, 8 * t : 8 * t + 8, LANES * j : LANES * j + LANES
                     ]
 
-    pl.semaphore_wait(barrier, PEERS + jnp.where((l == 0) | (l == LAT - 1), PEERS + LAT - 2, 2 * PEERS + LAT - 3))
+    relays = jnp.where((l == 3) | (l == 4), 5, jnp.where((l == 2) | (l == 5), 1, 2))
+    pl.semaphore_wait(barrier, PEERS + PEERS * jnp.where((l == 0) | (l == LAT - 1), 1, 2) + relays)
 
     def own_copy(k):
         return pltpu.make_async_remote_copy(
@@ -183,15 +180,11 @@
             device_id=(f, l + 1 - 2 * side), device_id_type=MESH,
         )
 
-    lower = l < LAT // 2
-    step = jnp.where(lower, l, LAT - 1 - l)
-    across = jnp.where(lower, LAT // 2, LAT // 2 - 1)
-
     def to_relay(c, side):
         read, _ = halo_rows(side)
         return pltpu.make_async_remote_copy(
             src_ref=T.at[0, c, pl.ds(read * 8, HALO * 8)], dst_ref=relay,
-            send_sem=relay_send.at[c], recv_sem=relay_recv.at[0],
+            send_sem=halo_send.at[side, c], recv_sem=relay_recv,
             device_id=(f, c if side == 0 else LAT - 1 - c), device_id_type=MESH,
         )
 
@@ -199,8 +192,8 @@
         _, land = halo_rows(side)
         return pltpu.make_async_remote_copy(
             src_ref=relay, dst_ref=T.at[0, c, pl.ds(land * 8, HALO * 8)],
-            send_sem=relay_send.at[3], recv_sem=halo_recv.at[side, c],
-            device_id=(f, across), device_id_type=MESH,
+            send_sem=relay_send, recv_sem=halo_recv.at[side, c],
+            device_id=(f, LAT // 2 - side), device_id_type=MESH,
         )
 
     def bytes_of(rows, sem):
@@ -249,61 +242,15 @@
 
     clear_edges()
 
-    for c in range(3):
-        for side in range(2):
-
-            @pl.when((step == c) & (lower if side == 0 else jnp.logical_not(lower)))
-            def _(c=c, side=side):
+    def pass_on(side):
+        for c in range(3):
+
+            @pl.when(l == (c if side == 0 else LAT - 1 - c))
+            def _(c=c):
                 to_relay(c, side).wait_recv()
                 from_relay(c, side).start()
 
-    bytes_of(4 * (PEERS - 1), own_recv).wait()
-    for side in range(2):
-
-        @pl.when(receives[side])
-        def _(side=side):
-            bytes_of(PEERS, edge_recv.at[side]).wait()
-
-    core_copy = pltpu.make_async_remote_copy(
-        src_ref=gathered.at[core], dst_ref=gathered.at[core], send_sem=core_send, recv_sem=core_recv,
-        device_id=partner, device_id_type=MESH,
-    )
-    core_copy.start()
-    core_copy.wait_recv()
-
-    def swap_groups(v):
-        v = list(v)
-        for bit in (1, 2, 4):
-            low = (group // bit) % 2 == 0
-            for a in range(8):
-                if not a & bit:
-                    lo, hi = v[a], v[a + bit]
-                    v[a] = jnp.where(low, lo, pltpu.roll(hi, GROUP * bit, 1))
-                    v[a + bit] = jnp.where(low, pltpu.roll(lo, LANES - GROUP * bit, 1), hi)
-        return v
-
-    for m, to in ((0, 8), (1, 16), (4, 0), (5, 24), (2, 32), (3, 40)):
-        rows = swap_groups([gathered[j % 2, j // 2, m] for j in range(8)])
-        for g in range(8):
-            slow[(to + g) * 8 : (to + g) * 8 + 8, :] = rows[g]
-
-    fetch_freq.wait()
-    frequency = freq_ref[0]
-
-    def coefficients(start, count, unroll):
-        def body(i, carry):
-            for u in range(unroll):
-                r = start + i * unroll + u
-                parts = node_phases(slow[at_row(r), :] * frequency)
-                for which in range(2):
-                    for n, value in enumerate(cosine_sums([p[which] for p in parts])):
-                        H[at_row(r * 16 + which * 8 + n), :] = value
-            return carry
-
-        lax.fori_loop(0, count // unroll, body, 0)
-
-    coefficients(1, 30, 5)
-    coefficients(32, 16, 4)
+    pass_on(1)
 
     def raise_rows(n, c, lo, hi, edge):
         B = hi - lo
@@ -330,6 +277,72 @@
                 if lo < hi:
                     for c in range(2):
                         raise_rows(n, 2 * pair + c, lo, hi, edge)
+
+    def first_levels(pair, carry):
+        for side in range(2):
+
+            @pl.when(receives[side])
+            def _(side=side):
+                for c in range(2):
+                    halo_copy(2 * pair + c, side).wait_recv()
+
+        levels(HALO, pair)
+        return carry
+
+    crossing = middle[0] | middle[1]
+
+    @pl.when(jnp.logical_not(crossing))
+    def _():
+        lax.fori_loop(0, 2, first_levels, 0)
+
+    bytes_of(4 * (PEERS - 1), own_recv).wait()
+    for side in range(2):
+
+        @pl.when(receives[side])
+        def _(side=side):
+            bytes_of(PEERS, edge_recv.at[side]).wait()
+
+    core_copy = pltpu.make_async_remote_copy(
+        src_ref=gathered.at[core], dst_ref=gathered.at[core], send_sem=core_send, recv_sem=core_recv,
+        device_id=partner, device_id_type=MESH,
+    )
+    core_copy.start()
+    pass_on(0)
+    core_copy.wait_recv()
+
+    def swap_groups(v):
+        v = list(v)
+        for bit in (1, 2, 4):
+            low = (group // bit) % 2 == 0
+            for a in range(8):
+                if not a & bit:
+                    lo, hi = v[a], v[a + bit]
+                    v[a] = jnp.where(low, lo, pltpu.roll(hi, GROUP * bit, 1))
+                    v[a + bit] = jnp.where(low, pltpu.roll(lo, LANES - GROUP * bit, 1), hi)
+        return v
+
+    for m, to in ((0, 8), (1, 16), (4, 0), (5, 24), (2, 32), (3, 40)):
+        rows = swap_groups([gathered[j % 2, j // 2, m] for j in range(8)])
+        for g in range(8):
+            slow[(to + g) * 8 : (to + g) * 8 + 8, :] = rows[g]
+
+    fetch_freq.wait()
+    frequency = freq_ref[0]
+
+    def coefficients(start, count, unroll):
+        def body(i, carry):
+            for u in range(unroll):
+                r = start + i * unroll + u
+                parts = node_phases(slow[at_row(r), :] * frequency)
+                for which in range(2):
+                    for n, value in enumerate(cosine_sums([p[which] for p in parts])):
+                        H[at_row(r * 16 + which * 8 + n), :] = value
+            return carry
+
+        lax.fori_loop(0, count // unroll, body, 0)
+
+    coefficients(1, 30, 5)
+    coefficients(32, 16, 4)
 
     def accumulate(start, lo, count, unroll):
         def body(i, carry):
@@ -395,18 +408,10 @@
                 row = row + pltpu.roll(row, turn, 1)
             img_ref[layer, 8 * m : 8 * m + 8, :] = row[:, :GROUP]
 
-    def first_levels(pair, carry):
-        for side in range(2):
-
-            @pl.when(receives[side])
-            def _(side=side):
-                for c in range(2):
-                    halo_copy(2 * pair + c, side).wait_recv()
-
-        levels(HALO, pair)
-        return carry
-
-    lax.fori_loop(0, 2, first_levels, 0)
+    @pl.when(crossing)
+    def _():
+        lax.fori_loop(0, 2, first_levels, 0)
+
     for side in range(2):
 
         @pl.when(sends[side] & jnp.logical_not(middle[side]))
@@ -420,7 +425,7 @@
                 to_relay(c, side).wait_send()
             halo_copy(3, side).wait_send()
 
-    @pl.when(step < 3)
+    @pl.when((l < LAT // 2 - 1) | (l > LAT // 2))
     def _():
         from_relay(0, 0).wait_send()
 
@@ -429,7 +434,6 @@
     image_terms(0)
 
     levels(HALO // 2, 0)
-    image_parts(0)
     levels(HALO // 2, 1)
     accumulate(32, TOP, 16, 4)
     image_terms(1)
@@ -444,6 +448,7 @@
         for i, ref in enumerate((src_out, rec_out))
     ]
     image_parts(1)
+    image_parts(0)
     for copy in stores:
         copy.start()
     image_sum(0)
@@ -463,11 +468,16 @@
     image_sum(1)
 
 
+def hand_on(*refs):
+    for i in range(3):
+        refs[3 + i][...] = refs[i][...]
+
+
 def migrate(frequencies, slowness, src_field, rec_field):
     f32 = jnp.float32
     field = jax.ShapeDtypeStruct(src_field.shape, f32)
     dma = pltpu.SemaphoreType.DMA
-    return pl.pallas_call(
+    outs = pl.pallas_call(
         kernel,
         out_shape=(jax.ShapeDtypeStruct(slowness.shape, f32), field, field),
         in_specs=[
@@ -500,7 +510,7 @@
             dma, dma,
             dma((2,)), dma((2,)),
             dma((2, 4)), dma((2, 4)),
-            dma((4,)), dma((4,)),
+            dma, dma,
             dma, dma,
             dma((2,)), dma((2,)),
             dma((2,)), dma((2,)),
@@ -508,6 +518,14 @@
         compiler_params=pltpu.CompilerParams(collective_id=0, has_side_effects=True, vmem_limit_bytes=64 << 20),
         name="migrate",
     )(frequencies, slowness, src_field, rec_field)
+    whole = [pl.BlockSpec(memory_space=pltpu.VMEM)] * 3
+    return pl.pallas_call(
+        hand_on,
+        out_shape=tuple(jax.ShapeDtypeStruct(out.shape, f32) for out in outs),
+        in_specs=whole,
+        out_specs=tuple(whole),
+        name="hand_on",
+    )(*outs)
 
 
 def solution(mesh):

time: 56.5 us -> 54 us (0.956)
  the two profiles are of different devices: /device:TPU:8 before, /device:TPU:24 now
where the time goes in v3:
time: 54 us; the launch traced here: 53.8 us
  Pallas kernels  52.5 us (97%)
  between operations  1.28 us (2%)
    pallas_call x1, Pallas kernels, migrate(): pl.pallas_call(kernel, out_shape=(jax.ShapeDtypeStruct(slowness.shape, f3...  50.8 us
    pallas_call x1, Pallas kernels, migrate(): pl.pallas_call(hand_on, out_shape=tuple((jax.ShapeDtypeStruct(out.shape,...  1.7 us

profile of v3, /device:TPU:24, one launch (start us, length us, event | category | flops | bytes accessed | tf_op | source)
XLA Modules:
  0.0 53.8 jit_solution(12557467356141712508)
XLA Ops:
  1.3 50.8 %migrate.1 = (f32[2,16,16]{2,1,0:T(8,128)}, f32[1,2,16,1024]{3,2,1,0:T(8,128)}, f32[1,2,16,1024]{3,2,1,0:T(8,128)}) custom-call(f32[1]{0:T(128)S(6)} %copy.7.freq_hbm, f32[2,16,16]{2,1,0:T(8,128)} %slow_hbm.1, f32[1,2,16,1024]{3,2,1,0:T(8,128)} %src_ref.1, f32[1,2,16,1024]{3,2,1,0:T(8,128)} %rec_ref.1), custom_call_target="tpu_custom_call" | custom-call | tf_op jit(solution)/shard_map/migrate/pallas_call | solution.py:480
  52.1 1.7 %hand_on.1 = (f32[2,16,16]{2,1,0:T(8,128)}, f32[1,2,16,1024]{3,2,1,0:T(8,128)}, f32[1,2,16,1024]{3,2,1,0:T(8,128)}) custom-call(f32[2,16,16]{2,1,0:T(8,128)} %get-tuple-element.6.refs_0_, f32[1,2,16,1024]{3,2,1,0:T(8,128)} %get-tuple-element.7.refs_1_, f32[1,2,16,1024]{3,2,1,0:T(8,128)} %get-tuple-element.8.refs_2_), custom_call_target="tpu_custom_call" | custom-call | tf_op jit(solution)/shard_map/hand_on/pallas_call | solution.py:522

commit v4 on v3

--- a/solution.py
+++ b/solution.py
@@ -203,30 +203,47 @@
     receives = [l > 0, l < LAT - 1]
 
     middle = [l == LAT // 2 - 1, l == LAT // 2]
-    for side in range(2):
-
-        @pl.when(middle[side])
-        def _(side=side):
-            for c in range(3):
-                to_relay(c, side).start()
-            halo_copy(3, side).start()
+    crossing = middle[0] | middle[1]
+
+    def edges_start(side):
+        for k in range(PEERS - 1, -1, -1):
+            edge_copy(k, side).start()
+
+    def relays_start(side):
+        for c in range(3):
+            to_relay(c, side).start()
+        halo_copy(3, side).start()
+
+    @pl.when(crossing)
+    def _():
+        edges_start(1)
+
+    @pl.when(middle[1])
+    def _():
+        relays_start(1)
 
     for k in range(PEERS - 1, 0, -1):
         own_copy(k).start()
-    for side in range(2):
-
-        @pl.when(sends[side])
-        def _(side=side):
-            for k in range(PEERS - 1, -1, -1):
-                edge_copy(k, side).start()
-
-    for side in range(2):
+
+    @pl.when(sends[1] & jnp.logical_not(crossing))
+    def _():
+        edges_start(1)
+
+    @pl.when(sends[0])
+    def _():
+        edges_start(0)
+
+    for side in (1, 0):
 
         @pl.when(sends[side] & jnp.logical_not(middle[side]))
         def _(side=side):
             for c in range(4):
                 halo_copy(c, side).start()
 
+    @pl.when(middle[0])
+    def _():
+        relays_start(0)
+
     for m in range(4):
         gathered[core, x, m, pl.ds(z, 1), :] = packed[m : m + 1, :]
 
@@ -253,9 +270,14 @@
     pass_on(1)
 
     def raise_rows(n, c, lo, hi, edge):
-        B = hi - lo
-        rows = pl.ds(lo * 8, B * 8)
-        v = T[n - 1, c, pl.ds((lo - 1) * 8, (B + 2) * 8), :].reshape(B + 2, 8, LANES)
+        raise_block(n, c, lo, hi - lo, edge)
+
+    def raise_block(n, c, lo, B, edge):
+        def span(row, count):
+            return pl.ds(row * 8 if isinstance(row, int) else pl.multiple_of(row * 8, 8), count * 8)
+
+        rows = span(lo, B)
+        v = T[n - 1, c, span(lo - 1, B + 2), :].reshape(B + 2, 8, LANES)
         e = v[:-1] + v[1:]
         q = e[:-1] + e[1:]
         stopped = jnp.where(corner[None], 0.0, q)
@@ -289,7 +311,34 @@
         levels(HALO, pair)
         return carry
 
-    crossing = middle[0] | middle[1]
+    def raise_split(pair, late):
+        for n in range(1, 8):
+            if late:
+                lo, count = jnp.where(middle[0], END - n, TOP - HALO + n), HALO
+            else:
+                lo, count = jnp.where(middle[0], TOP - HALO + n, TOP + n), TOP + HALO - 2 * n
+            for at in range(0, count, HALO):
+                for c in range(2):
+                    raise_block(n, 2 * pair + c, lo + at, min(HALO, count - at), None)
+
+    def split_levels(late):
+        def body(pair, carry):
+            for m in range(2):
+
+                @pl.when(middle[m])
+                def _(m=m):
+                    for c in range(2):
+                        halo_copy(2 * pair + c, 1 - m if late else m).wait_recv()
+
+            raise_split(pair, late)
+            return carry
+
+        lax.fori_loop(0, 2, body, 0)
+
+
+    @pl.when(crossing)
+    def _():
+        split_levels(False)
 
     @pl.when(jnp.logical_not(crossing))
     def _():
@@ -410,7 +459,7 @@
 
     @pl.when(crossing)
     def _():
-        lax.fori_loop(0, 2, first_levels, 0)
+        split_levels(True)
 
     for side in range(2):
 

time: 54 us -> 49.5 us (0.917)
  Pallas kernels: 52.5 us -> 47.8 us
    pallas_call x1, Pallas kernels: 50.8 us -> 46.1 us  [migrate(): pl.pallas_call(kernel, out_shape=(jax.ShapeDtypeStruct(slowness.shape, f3...]
where the time goes in v4:
time: 49.5 us; the launch traced here: 49.1 us
  Pallas kernels  47.8 us (97%)
  between operations  1.28 us (3%)
    pallas_call x1, Pallas kernels, migrate(): pl.pallas_call(kernel, out_shape=(jax.ShapeDtypeStruct(slowness.shape, f3...  46.1 us
    pallas_call x1, Pallas kernels, migrate(): pl.pallas_call(hand_on, out_shape=tuple((jax.ShapeDtypeStruct(out.shape,...  1.7 us

profile of v4, /device:TPU:24, one launch (start us, length us, event | category | flops | bytes accessed | tf_op | source)
XLA Modules:
  0.0 49.1 jit_solution(12882514842429043879)
XLA Ops:
  1.3 46.1 %migrate.1 = (f32[2,16,16]{2,1,0:T(8,128)}, f32[1,2,16,1024]{3,2,1,0:T(8,128)}, f32[1,2,16,1024]{3,2,1,0:T(8,128)}) custom-call(f32[1]{0:T(128)S(6)} %copy.7.freq_hbm, f32[2,16,16]{2,1,0:T(8,128)} %slow_hbm.1, f32[1,2,16,1024]{3,2,1,0:T(8,128)} %src_ref.1, f32[1,2,16,1024]{3,2,1,0:T(8,128)} %rec_ref.1), custom_call_target="tpu_custom_call" | custom-call | tf_op jit(solution)/shard_map/migrate/pallas_call | solution.py:529
  47.4 1.7 %hand_on.1 = (f32[2,16,16]{2,1,0:T(8,128)}, f32[1,2,16,1024]{3,2,1,0:T(8,128)}, f32[1,2,16,1024]{3,2,1,0:T(8,128)}) custom-call(f32[2,16,16]{2,1,0:T(8,128)} %get-tuple-element.6.refs_0_, f32[1,2,16,1024]{3,2,1,0:T(8,128)} %get-tuple-element.7.refs_1_, f32[1,2,16,1024]{3,2,1,0:T(8,128)} %get-tuple-element.8.refs_2_), custom_call_target="tpu_custom_call" | custom-call | tf_op jit(solution)/shard_map/hand_on/pallas_call | solution.py:571
